TPU v7x, 32 devices: a whole 2x2x4 slice. The times are simulated.
32 devices in a mesh: groups: 2 (over y), dp: 4 (over z), expert: 4 (over x, core).
Axes of the slice: x: 2, y: 2, z: 4, core: 2. Of those that a mesh axis runs over, the one named last changes fastest.
Arguments:
- output_gradient: bfloat16 [1024, 3072], P(('groups', 'dp'), 'expert'), parts along dimension 0, may hold values from -6 to 6
- hidden: bfloat16 [4, 1024, 8192], P('expert', 'groups', 'dp'), parts along dimension 1, may hold values from -0.59765625 to 0.59765625
- down_matrix: bfloat16 [4, 8192, 3072], P('expert', 'dp'), may hold values from -0.0625 to 0.0625
- adapter_down_matrix: bfloat16 [4, 8192, 512], P('expert', 'dp'), may hold values from -0.0625 to 0.0625
- adapter_up_matrix: bfloat16 [4, 512, 3072], P('expert', None, 'dp'), may hold values from -0.109375 to 0.109375
- routes: int32 [1024, 2], P(('groups', 'dp')), parts along dimension 0, may hold values from 0 to 3, all different within a row; in each aligned block of 128 rows (0 to 127, 128 to 255, ...) at most 128 rows name the same one
- router_weight: bfloat16 [1024, 2], P(('groups', 'dp')), parts along dimension 0, may hold values from 0.099609375 to 0.8984375
- tenant: int32 [1024], P(('groups', 'dp')), parts along dimension 0, may hold values from 0 to 15
Outputs:
- hidden_gradient: bfloat16 [4, 1024, 8192], P('expert', 'groups', 'dp'), parts along dimension 1
- adapter_down_gradient: float32 [8, 8192, 512], P(('groups', 'expert'), 'dp'), parts along dimension 0
- adapter_up_gradient: float32 [8, 512, 3072], P(('groups', 'expert'), None, 'dp'), parts along dimension 0
- router_gradient: float32 [1024, 2], P(('groups', 'dp')), parts along dimension 0
There are 2 independent parts, one for each index of `groups`. A program takes and returns all parts, laid end to end along the dimension named above; an argument that names none is the same for every part. Nothing has to cross between parts.
Inputs may be any that keep to these rules, and one draw needn't show every extreme that they name: `routes`: within the 128 tokens of one index of dp no expert is named more than 128 times, and in some such block an expert is named exactly 128 times; the two experts of a token differ.
All inputs are finite; a program needn't handle non-finite values.
Results may differ from a plain program's by a relative error of at most 0.0029.
Values may be sent and summed in bfloat16 or wider, within the bound.
A program may use at most 128 MiB of HBM per device.

v0:
```python
import jax
import jax.numpy as jnp
from jax import lax
from jax.sharding import PartitionSpec as P

ADAPTER_RANK = 32
TENANT_COUNT = 16


adapter_scale = 2.0


def slot_places(routes, experts, capacity):
    sources = routes.shape[0]
    flattened = routes.reshape(sources, -1)
    expert_hits = (
        flattened[:, :, None] == jnp.arange(experts, dtype=jnp.int32)[None, None, :]
    ).astype(jnp.int32)
    earlier = jnp.cumsum(expert_hits, axis=1) - expert_hits
    offset = jnp.sum(earlier * expert_hits, axis=2)
    target = flattened * capacity + offset
    return target[:, None, :] == jnp.arange(experts * capacity, dtype=jnp.int32)[None, :, None]


def tenant_mask(owner):
    return (owner[:, None] == jnp.arange(TENANT_COUNT, dtype=jnp.int32)[None, :]).astype(
        jnp.float32
    )


def select_rank_columns(matrix, owning_tenants):
    return jnp.sum(
        matrix.reshape(owning_tenants.shape[0], TENANT_COUNT, ADAPTER_RANK)
        * owning_tenants[:, :, None],
        axis=1,
    )


def expand_rank(values, owning_tenants):
    return (owning_tenants[:, :, None] * values[:, None, :]).reshape(
        owning_tenants.shape[0], TENANT_COUNT * ADAPTER_RANK
    )


def contract_matrices(left, right, left_dim, right_dim):
    return lax.dot_general(
        left, right, (((left_dim,), (right_dim,)), ((), ())), preferred_element_type=jnp.float32
    )


def rows_terms(
    dispatched,
    weight_slot,
    owner_slot,
    hidden_activation_rows,
    down_rows,
    adapter_input,
    adapter_output,
    shard_index,
):
    owning_tenants = tenant_mask(owner_slot)
    block_width = adapter_output.shape[1]
    feature_tile = lax.dynamic_slice_in_dim(dispatched, shard_index * block_width, block_width, 1)
    frozen_gradient = contract_matrices(dispatched, down_rows, 1, 1)
    inner_left_factor = select_rank_columns(
        jnp.dot(hidden_activation_rows, adapter_input, preferred_element_type=jnp.float32),
        owning_tenants,
    )
    inner_right_factor = select_rank_columns(
        contract_matrices(feature_tile, adapter_output, 1, 1), owning_tenants
    )
    partial_score = jnp.sum(hidden_activation_rows.astype(jnp.float32) * frozen_gradient, axis=1)
    return (
        frozen_gradient,
        inner_left_factor,
        inner_right_factor,
        partial_score,
        weight_slot.astype(jnp.float32),
        owner_slot,
        feature_tile,
    )


def body(
    output_gradient,
    hidden,
    down_matrix,
    adapter_down_matrix,
    adapter_up_matrix,
    routes,
    router_weight,
    tenant,
):
    experts = lax.axis_size("expert")
    expert_index = lax.axis_index("expert")
    shard_index = lax.axis_index("dp")
    token_count = output_gradient.shape[0]
    capacity = 4 * token_count // experts
    hidden_activation_rows = hidden[0]
    down_rows = down_matrix[0]
    adapter_input = adapter_down_matrix[0]
    adapter_output = adapter_up_matrix[0]
    own_table = slot_places(routes[None], experts, capacity)[0]
    token_match = (
        own_table.reshape(experts * capacity, token_count, 2).astype(jnp.bfloat16).sum(axis=2)
    )
    outgoing = jnp.dot(token_match, output_gradient, preferred_element_type=jnp.float32).astype(
        jnp.bfloat16
    )
    outgoing = outgoing.reshape(experts, capacity, -1)
    arrived = lax.all_to_all(outgoing, "expert", split_axis=0, concat_axis=2, tiled=True)[0]
    chosen = lax.dynamic_slice_in_dim(own_table, expert_index * capacity, capacity, 0)
    weight_slot = jnp.sum(
        jnp.where(chosen, router_weight.reshape(1, -1).astype(jnp.float32), 0.0), axis=1
    ).astype(jnp.bfloat16)
    owner_slot = jnp.sum(jnp.where(chosen, jnp.repeat(tenant, 2)[None, :], 0), axis=1)
    portion = lax.all_gather((arrived, weight_slot, owner_slot), "dp", axis=0, tiled=True)
    results = rows_terms(
        portion[0],
        portion[1],
        portion[2],
        hidden_activation_rows,
        down_rows,
        adapter_input,
        adapter_output,
        shard_index,
    )
    (
        frozen_gradient,
        inner_left_factor,
        inner_right_factor,
        partial_score,
        weight_float,
        owner_all,
        feature_tile,
    ) = results
    inner_left_factor, inner_right_factor = lax.psum((inner_left_factor, inner_right_factor), "dp")
    owned_score = lax.psum_scatter(partial_score, "dp", scatter_dimension=0, tiled=True)
    owned_left_factor = lax.dynamic_slice_in_dim(
        inner_left_factor, shard_index * capacity, capacity, 0
    )
    owned_right_factor = lax.dynamic_slice_in_dim(
        inner_right_factor, shard_index * capacity, capacity, 0
    )
    owned_score = owned_score + adapter_scale * jnp.sum(
        owned_left_factor * owned_right_factor, axis=1
    )
    returned = lax.all_gather(owned_score, "expert", axis=0, tiled=True)
    router_gradient = jnp.sum(jnp.where(own_table, returned[:, None], 0.0), axis=0).reshape(
        token_count, 2
    )
    owning_tenants = tenant_mask(owner_all)
    scale_factor = weight_float[:, None]
    spread_right_factor = expand_rank(inner_right_factor, owning_tenants)
    scaled_right_factor = (scale_factor * spread_right_factor).astype(jnp.bfloat16)
    scaled_left_factor = (scale_factor * expand_rank(inner_left_factor, owning_tenants)).astype(
        jnp.bfloat16
    )
    adapter_contribution = contract_matrices(
        spread_right_factor.astype(jnp.bfloat16), adapter_input, 1, 1
    )
    hidden_gradient = (
        scale_factor * (frozen_gradient + adapter_scale * adapter_contribution)
    ).astype(jnp.bfloat16)
    first_route_gradient = adapter_scale * contract_matrices(
        hidden_activation_rows, scaled_right_factor, 0, 0
    )
    second_route_gradient = adapter_scale * contract_matrices(
        scaled_left_factor, feature_tile, 0, 0
    )
    return (
        hidden_gradient[None],
        first_route_gradient[None],
        second_route_gradient[None],
        router_gradient,
    )


def solution(mesh):
    in_specs = (
        P(("groups", "dp"), "expert"),
        P("expert", "groups", "dp"),
        P("expert", "dp", None),
        P("expert", "dp", None),
        P("expert", None, "dp"),
        P(("groups", "dp"), None),
        P(("groups", "dp"), None),
        P(("groups", "dp")),
    )
    out_specs = (
        P("expert", "groups", "dp"),
        P(("groups", "expert"), "dp", None),
        P(("groups", "expert"), None, "dp"),
        P(("groups", "dp"), None),
    )
    return jax.shard_map(body, mesh=mesh, in_specs=in_specs, out_specs=out_specs, check_vma=False)
```

profile of v0, /device:TPU:0, one launch (start us, length us, event | category | flops | bytes accessed | tf_op | source)
XLA Modules:
  0.0 164.7 jit_solution(2782207650247495027)
XLA Ops:
  7.2 0.0 copy-start
  7.2 0.0 all-gather.5.cloned.1.call-start
  7.2 0.9 copy.49
  8.1 0.1 reshape_broadcast_in_dim.3
  8.2 1.2 reduce-window.6
  9.5 0.1 slice.8
  9.6 0.1 copy.50
  9.7 0.1 copy.51
  9.8 0.1 broadcast.150
  9.9 0.1 reduce_sum.88
  10.1 0.1 copy.53
  10.1 0.7 multiply_add_fusion
  10.8 0.1 fusion.20
  10.9 0.0 copy-start.3
  10.9 0.0 copy-start.4
  10.9 1.3 convolution_convert_fusion
  12.2 0.0 copy-start.1
  12.2 15.8 %all_to_all.15 = bf16[4,128,768]{2,1,0:T(8,128)(2,1)S(1)} all-to-all(bf16[4,128,768]{2,1,0:T(8,128)(2,1)S(1)} %bitcast.82), channel_id=1, replica_groups=mesh['groups'=2,'dp'=4,'expert'=4] {'expert'}, dimensions={0} | all-to-all | bytes 1572864 | tf_op jit(solution)/shard_map/all_to_all | solution.py:111
  28.0 0.6 copy.54
  28.6 0.0 copy-start.5
  28.6 1.0 copy.58
  29.6 0.0 all-gather.5.cloned.1.call-update
  29.6 0.0 all-reduce.4.cloned.1.call-start
  29.7 0.0 copy-done.3
  29.7 0.1 copy.52
  29.8 0.1 reshape.288
  30.0 0.0 copy-done.4
  30.0 0.1 broadcast_in_dim.67
  30.1 0.1 broadcast_in_dim.68
  30.2 0.1 select_reduce_fusion.2
  30.3 11.1 %all-gather = bf16[4,1,128]{2,1,0:T(2,128)(2,1)S(1)} all-gather(bf16[1,1,128]{2,1,0:T(2,128)(2,1)S(1)} %bitcast.95), channel_id=1, replica_groups=mesh['groups'=2,'dp'=4,'expert'=4] {'dp'}, dimensions={0}, use_global_device_ids=true | all-gather | bytes 1280 | tf_op jit(solution)/shard_map/all_gather | solution.py:117
  41.5 0.0 copy-done.1
  41.5 2.4 %copy.55 = bf16[1,2048,512]{1,2,0:T(8,128)(2,1)} copy(bf16[1,2048,512]{2,1,0:T(8,128)(2,1)S(1)} %copy-done.1) | data formatting | bytes 4194304 | tf_op args[3]
  43.8 0.0 copy-done.5
  43.8 0.6 dynamic-slice.1
  45.1 0.1 select_reduce_fusion.1
  45.2 7.6 %all-gather.1 = s32[4,1,128]{2,1,0:T(1,128)S(1)} all-gather(s32[1,1,128]{2,1,0:T(1,128)S(1)} %bitcast.94), channel_id=1, replica_groups=mesh['groups'=2,'dp'=4,'expert'=4] {'dp'}, dimensions={0}, use_global_device_ids=true | all-gather | bytes 2560 | tf_op jit(solution)/shard_map/all_gather | solution.py:117
  52.8 4.2 %fusion.10 = f32[512,32]{0,1:T(8,128)} fusion(bf16[16,32,2048]{2,1,0:T(8,128)(2,1)} %bitcast.86, bf16[1,512,2048]{2,1,0:T(8,128)(2,1)} %param.9, f32[512,16]{0,1:T(8,128)S(1)} %fusion.22), kind=kOutput, calls=%fused_computation.16 | convolution fusion | flops 1074249728 | bytes 4292608 | tf_op jit(solution)/shard_map/dot_general | solution.py:66
  56.9 36.7 %all-gather.5.cloned.1.call-done = bf16[512,3072]{1,0:T(8,128)(2,1)} async-done(((bf16[128,3072]{1,0:T(8,128)(2,1)}), bf16[512,3072]{1,0:T(8,128)(2,1)}) %all-gather.5.cloned.1.call-update) | async-done | bytes 3145744 | tf_op jit(solution)/shard_map/all_gather | solution.py:117
  93.7 0.0 copy-done
  93.7 2.4 %fusion.13 = f32[512,32]{0,1:T(8,128)} fusion(bf16[16,32,768]{2,1,0:T(8,128)(2,1)S(1)} %bitcast.80, bf16[512,3072]{1,0:T(8,128)(2,1)} %all-gather.5.cloned.1.call-done, s32[]{:T(128)S(6)} %select_n.25, f32[512,16]{0,1:T(8,128)S(1)} %fusion.22), kind=kOutput, calls=%fused_computation.17 | convolution fusion | flops 403161088 | bytes 1671172 | tf_op jit(solution)/shard_map/dot_general | solution.py:46
  96.0 0.0 all-reduce.4.cloned.1.call-update
  96.1 12.4 %multiply_reduce_fusion = (f32[512]{0:T(512)S(1)}, f32[512,2048]{1,0:T(8,128)}) fusion(bf16[1,512,2048]{2,1,0:T(8,128)(2,1)} %param.9, bf16[512,3072]{1,0:T(8,128)(2,1)} %all-gather.5.cloned.1.call-done, bf16[1,2048,3072]{2,1,0:T(8,128)(2,1)} %param.10), kind=kOutput, calls=%fused_computation.2 | convolution fusion | flops 6445596160 | bytes 22022144 | tf_op jit(solution)/shard_map/dot_general | solution.py:46
  108.4 9.1 %all-reduce = f32[512]{0:T(512)S(1)} all-reduce(f32[512]{0:T(512)S(1)} %get-tuple-element.29), channel_id=2, replica_groups=mesh['groups'=2,'dp'=4,'expert'=4] {'dp'}, use_global_device_ids=true, to_apply=%region_11.12.clone | all-reduce | flops 512 | bytes 4096
  117.5 12.3 %all-reduce.4.cloned.1.call-done = (f32[512,32]{0,1:T(8,128)}, f32[512,32]{0,1:T(8,128)}) async-done(((f32[512,32]{0,1:T(8,128)}, f32[512,32]{0,1:T(8,128)}), (f32[512,32]{0,1:T(8,128)}, f32[512,32]{0,1:T(8,128)})) %all-reduce.4.cloned.1.call-update) | async-done | bytes 131088 | tf_op jit(solution)/shard_map/psum | solution.py:137
  129.8 0.8 multiply_reduce_fusion.1
  130.6 1.9 %fusion.14 = (bf16[512,16,32]{0,2,1:T(8,128)(2,1)}, bf16[512,16,32]{0,2,1:T(8,128)(2,1)S(1)}, f32[512,16,32]{0,2,1:T(8,128)S(1)}) fusion(f32[512]{0:T(512)S(1)} %bitcast.88, f32[512,32]{0,1:T(8,128)} %get-tuple-element.24, f32[512,16]{0,1:T(8,128)S(1)} %fusion.22, f32[512,32]{0,1:T(8,128)} %get-tuple-element.25), kind=kLoop, calls=%fused_computation.18 | loop fusion | flops 1310720 | bytes 2263040 | tf_op jit(solution)/shard_map/convert_element_type | solution.py:155
  132.5 0.9 fusion.15
  133.4 0.1 fusion.27
  133.5 5.0 %all-gather.2 = f32[4,1,128]{2,1,0:T(1,128)S(1)} all-gather(f32[1,1,128]{2,1,0:T(1,128)S(1)} %fusion.27), channel_id=1, replica_groups=mesh['groups'=2,'dp'=4,'expert'=4] {'expert'}, dimensions={0}, use_global_device_ids=true | all-gather | bytes 2560 | tf_op jit(solution)/shard_map/all_gather | solution.py:148
  138.5 0.1 select_reduce_fusion
  138.7 0.1 reshape.287
  138.8 0.6 copy.57
  139.4 5.0 %multiply_bitcast_fusion = f32[1,2048,512]{1,2,0:T(8,128)} fusion(bf16[512,512]{0,1:T(8,128)(2,1)} %bitcast.87, bf16[1,512,2048]{2,1,0:T(8,128)(2,1)} %param.9), kind=kOutput, calls=%fused_computation.3 | convolution fusion | flops 1074790400 | bytes 6815744 | tf_op jit(solution)/shard_map/dot_general | solution.py:46
  144.4 5.3 %copy.56 = f32[1,2048,512]{2,1,0:T(8,128)} copy(f32[1,2048,512]{1,2,0:T(8,128)} %multiply_bitcast_fusion) | data formatting | bytes 8388608
  149.8 0.0 copy-start.2
  149.8 5.3 %fusion.2 = bf16[1,512,2048]{2,1,0:T(8,128)(2,1)} fusion(f32[512,2048]{1,0:T(8,128)} %get-tuple-element.30, bf16[512,512]{0,1:T(8,128)(2,1)S(1)} %bitcast.85, bf16[1,2048,512]{2,1,0:T(8,128)(2,1)S(1)} %copy-done.1, f32[512]{0:T(512)S(1)} %bitcast.90), kind=kOutput, calls=%fused_computation.5 | convolution fusion | flops 1077936128 | bytes 8914944 | tf_op jit(solution)/shard_map/dot_general | solution.py:46
  155.0 0.0 copy-done.2
  155.0 2.8 %multiply_bitcast_fusion.1 = f32[1,512,768]{2,1,0:T(8,128)} fusion(bf16[512,512]{0,1:T(8,128)(2,1)S(1)} %copy-done.2, bf16[512,3072]{1,0:T(8,128)(2,1)} %all-gather.5.cloned.1.call-done, s32[]{:T(128)S(6)} %select_n.25), kind=kOutput, calls=%fused_computation.10 | convolution fusion | flops 403046400 | bytes 2883588 | tf_op jit(solution)/shard_map/dot_general | solution.py:46
  (10 shorter events, 0.1 us)
Async XLA Ops:
  7.2 86.5 %copy-start = (bf16[1,512,768]{2,1,0:T(8,128)(2,1)S(1)}, bf16[1,512,768]{2,1,0:T(8,128)(2,1)}, u32[]{:S(2)}) copy-start(bf16[1,512,768]{2,1,0:T(8,128)(2,1)} %param.12) | copy-start | bytes 2359300
  7.2 86.5 %all-gather.5.cloned.1.call-start = ((), (), s32[]{:S(2)}) async-start(), calls=%async_computation.1 | async-start | bytes 3932160 | tf_op jit(solution)/shard_map/all_gather | solution.py:117
  10.9 18.8 %copy-start.3 = (bf16[128,2]{0,1:T(2,128)(2,1)S(1)}, bf16[128,2]{0,1:T(2,128)(2,1)}, u32[]{:S(2)}) copy-start(bf16[128,2]{0,1:T(2,128)(2,1)} %param.14) | copy-start | bytes 1540
  10.9 19.1 %copy-start.4 = (s32[128]{0:T(128)S(1)}, s32[128]{0:T(128)}, u32[]{:S(2)}) copy-start(s32[128]{0:T(128)} %param.15) | copy-start | bytes 1540
  12.2 29.3 %copy-start.1 = (bf16[1,2048,512]{2,1,0:T(8,128)(2,1)S(1)}, bf16[1,2048,512]{2,1,0:T(8,128)(2,1)}, u32[]{:S(2)}) copy-start(bf16[1,2048,512]{2,1,0:T(8,128)(2,1)} %param.11) | copy-start | bytes 6291460
  28.6 15.2 %copy-start.5 = (u32[32]{0:T(128)S(1)}, u32[32]{0:T(128)}, u32[]{:S(2)}) copy-start(u32[32]{0:T(128)} %constant.38) | copy-start | bytes 388
  29.6 100.2 %all-reduce.4.cloned.1.call-start = ((), (), s32[]{:S(2)}) async-start(), calls=%async_computation.2 | async-start | bytes 262144 | tf_op jit(solution)/shard_map/psum | solution.py:137
  149.8 5.3 %copy-start.2 = (bf16[512,512]{0,1:T(8,128)(2,1)S(1)}, bf16[512,512]{0,1:T(8,128)(2,1)}, u32[]{:S(2)}) copy-start(bf16[512,512]{0,1:T(8,128)(2,1)} %fusion.15) | copy-start | bytes 1572868
Sparse Core Ops, SparseCore 0:
  29.8 63.8 all-gather.4
  96.6 33.1 all-reduce.3
where the time goes:
time: 165 us
  waiting for transfers between devices  49.1 us (30%)
  blocking collectives  48.6 us (29%)
  matrix products  33.3 us (20%)
  between operations  14.8 us (9%)
  local copies, waits for them, and re-layouts  12.8 us (8%)
  other arithmetic  6.11 us (4%)
    all_gather x1, waiting for transfers between devices, body(): lax.all_gather((arrived, weight_slot, owner_slot), 'dp', axis=0, tiled=True)  36.7 us
    dot_general x5, matrix products, contract_matrices(): lax.dot_general(left, right, (((left_dim,), (right_dim,)), ((), ())), pre...  27.8 us
    all_gather x2, blocking collectives, body(): lax.all_gather((arrived, weight_slot, owner_slot), 'dp', axis=0, tiled=True)  18.7 us
    all_to_all x1, blocking collectives, body(): lax.all_to_all(outgoing, 'expert', split_axis=0, concat_axis=2, tiled=True)  15.8 us
    psum x1, waiting for transfers between devices, body(): lax.psum((inner_left_factor, inner_right_factor), 'dp')  12.3 us
    unnamed x18, local copies, waits for them, and re-layouts  10.8 us
    unnamed x1, blocking collectives  9.05 us
    all_gather x1, blocking collectives, body(): returned = lax.all_gather(owned_score, 'expert', axis=0, tiled=True)  5.03 us
  transfers between devices with their start and end apart: 2, of which 2 were waited for; matrix products, arithmetic and copies ran while one was open for 12% of the time, Pallas kernels for 0%

commit v1 on v0

--- a/solution.py
+++ b/solution.py
@@ -1,6 +1,10 @@
+import functools
+
 import jax
 import jax.numpy as jnp
 from jax import lax
+from jax.experimental import pallas as pl
+from jax.experimental.pallas import tpu as pltpu
 from jax.sharding import PartitionSpec as P
 
 ADAPTER_RANK = 32
@@ -176,6 +180,657 @@
     )
 
 
+MESH = pl.DeviceIdType.MESH
+LANES = 128
+
+
+def dot_nt(left, right):
+    return contract_matrices(left, right, 1, 1)
+
+
+def fold_lanes(values, owners):
+    lane_group = lax.broadcasted_iota(jnp.int32, owners.shape, 1) // ADAPTER_RANK
+    total = jnp.zeros(owners.shape, jnp.float32)
+    for part in range(TENANT_COUNT * ADAPTER_RANK // LANES):
+        mine = owners == (lane_group + part * (LANES // ADAPTER_RANK)).astype(jnp.float32)
+        total = total + jnp.where(mine, values[:, part * LANES : (part + 1) * LANES], 0.0)
+    return repeat_groups(total)
+
+
+def repeat_groups(values):
+    values = values + pltpu.roll(values, 2 * ADAPTER_RANK, 1)
+    return values + pltpu.roll(values, ADAPTER_RANK, 1)
+
+
+def pack_rows(values):
+    rows = values.shape[0] // 4
+    lane_group = lax.broadcasted_iota(jnp.int32, (rows, LANES), 1) // ADAPTER_RANK
+    total = values[:rows]
+    for part in range(1, 4):
+        total = jnp.where(lane_group == part, values[part * rows : (part + 1) * rows], total)
+    return total
+
+
+def unpack_rows(values):
+    lane_group = lax.broadcasted_iota(jnp.int32, values.shape, 1) // ADAPTER_RANK
+    return jnp.concatenate(
+        [repeat_groups(jnp.where(lane_group == part, values, 0.0)) for part in range(4)], axis=0
+    )
+
+
+def spread_rows(values, owners):
+    lane_group = lax.broadcasted_iota(jnp.int32, owners.shape, 1) // ADAPTER_RANK
+    parts = []
+    for part in range(TENANT_COUNT * ADAPTER_RANK // LANES):
+        mine = owners == (lane_group + part * (LANES // ADAPTER_RANK)).astype(jnp.float32)
+        parts.append(jnp.where(mine, values, 0.0))
+    return jnp.concatenate(parts, axis=1)
+
+
+def kernel(
+    tiles,
+    grad_ref,
+    hidden_ref,
+    down_ref,
+    adown_ref,
+    aup_ref,
+    routes_ref,
+    weight_ref,
+    tenant_ref,
+    hgrad_out,
+    dgrad_out,
+    ugrad_out,
+    router_out,
+    tok,
+    disp,
+    down_v,
+    hid,
+    hid_t,
+    ain,
+    aup,
+    base,
+    hg_v,
+    dg_v,
+    ug_v,
+    u_acc,
+    meta,
+    place,
+    w_row,
+    own_row,
+    u_buf,
+    v_buf,
+    u_sum,
+    v_sum,
+    sp_v,
+    sc_v,
+    sc_ut,
+    score_acc,
+    score_out,
+    score_in,
+    final_out,
+    final_in,
+    tok_recv,
+    send_z,
+    send_x,
+    send_c,
+    meta_send,
+    meta_recv,
+    u_send,
+    u_recv,
+    v_send,
+    v_recv,
+    score_send,
+    score_recv,
+    final_send,
+    final_recv,
+    load_sem,
+    down_sem,
+    hid_sem,
+    out_sem,
+    out_sem_hg,
+    out_sem_dg,
+):
+    me = lax.axis_index("dp")
+    expert = lax.axis_index("expert")
+    across = lax.rem(expert + 2, 4)
+    core = expert + 1 - 2 * lax.rem(expert, 2)
+    diagonal = lax.rem(core + 2, 4)
+    near = me // 2
+    far = 1 - near
+    width = hid.shape[2]
+    f32 = jnp.float32
+    bf16 = jnp.bfloat16
+
+    own_copy = pltpu.make_async_copy(grad_ref, tok.at[expert, me], load_sem.at[0])
+    ain_copy = pltpu.make_async_copy(adown_ref.at[0], ain, load_sem.at[1])
+    aup_copy = pltpu.make_async_copy(aup_ref.at[0], aup, load_sem.at[2])
+    hid_copies = [
+        pltpu.make_async_copy(
+            hidden_ref.at[0, :, pl.ds(j * width, width)], hid.at[j], hid_sem.at[j]
+        )
+        for j in range(tiles)
+    ]
+    down_copies = [
+        pltpu.make_async_copy(
+            down_ref.at[0, pl.ds(j * width, width), :], down_v.at[j], down_sem.at[j]
+        )
+        for j in range(tiles)
+    ]
+    own_copy.start()
+    for copy in hid_copies:
+        copy.start()
+    ain_copy.start()
+    aup_copy.start()
+    for copy in down_copies:
+        copy.start()
+    meta[me, 0:2, :] = routes_ref[...].astype(f32)
+    meta[me, 2:4, :] = weight_ref[...].astype(f32)
+    meta[me, 4:5, :] = tenant_ref[...].astype(f32)
+    meta[me, 5:8, :] = jnp.zeros((3, LANES), f32)
+
+    barrier = pltpu.get_barrier_semaphore()
+    for step in range(1, 4):
+        pl.semaphore_signal(
+            barrier, inc=1, device_id={"dp": lax.rem(me + step, 4)}, device_id_type=MESH
+        )
+        pl.semaphore_signal(
+            barrier, inc=1, device_id={"expert": lax.rem(expert + step, 4)}, device_id_type=MESH
+        )
+    pl.semaphore_wait(barrier, 6)
+
+    def remote(src, dst, send, recv, **target):
+        return pltpu.make_async_remote_copy(
+            src_ref=src,
+            dst_ref=dst,
+            send_sem=send,
+            recv_sem=recv,
+            device_id=target,
+            device_id_type=MESH,
+        )
+
+    def to_left(p, src=None):
+        block = tok.at[expert, p]
+        return remote(
+            block if src is None else src,
+            block,
+            send_z.at[0, p],
+            tok_recv.at[expert, p],
+            dp=jnp.maximum(me - 1, 0),
+        )
+
+    def to_right(p, src=None):
+        block = tok.at[expert, p]
+        return remote(
+            block if src is None else src,
+            block,
+            send_z.at[1, p],
+            tok_recv.at[expert, p],
+            dp=jnp.minimum(me + 1, 3),
+        )
+
+    def to_across(p, src=None):
+        block = tok.at[expert, p]
+        return remote(
+            block if src is None else src,
+            block,
+            send_x.at[p],
+            tok_recv.at[expert, p],
+            expert=across,
+        )
+
+    def to_core(q, slot, p, src=None):
+        block = tok.at[q, p]
+        return remote(
+            block if src is None else src,
+            block,
+            send_c.at[slot, p],
+            tok_recv.at[q, p],
+            expert=core,
+        )
+
+    def arrived(q, p):
+        block = tok.at[q, p]
+        remote(block, block, send_c.at[0, p], tok_recv.at[q, p], expert=core).wait_recv()
+
+    meta_copies = []
+    for step in range(1, 4):
+        copy = remote(
+            meta.at[me],
+            meta.at[me],
+            meta_send.at[step - 1],
+            meta_recv.at[me],
+            dp=lax.rem(me + step, 4),
+        )
+        copy.start()
+        meta_copies.append(copy)
+
+    @pl.when(me > 0)
+    def _():
+        to_left(me, grad_ref).start()
+
+    @pl.when(me < 3)
+    def _():
+        to_right(me, grad_ref).start()
+
+    to_across(me, grad_ref).start()
+    to_core(expert, 0, me, grad_ref).start()
+
+    for step in range(1, 4):
+        p = lax.rem(me + step, 4)
+        remote(
+            meta.at[p], meta.at[p], meta_send.at[0], meta_recv.at[p], dp=p
+        ).wait_recv()
+    expert_f = expert.astype(f32)
+    row_ids = lax.broadcasted_iota(jnp.int32, (LANES, LANES), 0)
+    col_ids = lax.broadcasted_iota(jnp.int32, (LANES, LANES), 1)
+    before = (row_ids < col_ids).astype(bf16)
+    for p in range(4):
+        info = meta[p]
+        first = info[0:1] == expert_f
+        second = info[1:2] == expert_f
+        hit = jnp.where(first | second, 1.0, 0.0)
+        offset = jnp.dot(
+            jnp.broadcast_to(hit, (16, LANES)).astype(bf16), before, preferred_element_type=f32
+        )[0:1]
+        offset = jnp.where(hit > 0.0, offset, -1.0)
+        table = offset == row_ids.astype(f32)
+        place[p] = jnp.where(table, 1.0, 0.0).astype(bf16)
+        chosen = jnp.where(first, info[2:3], info[3:4])
+        rows = pl.ds(p * LANES, LANES)
+        w_row[rows] = jnp.broadcast_to(
+            jnp.sum(jnp.where(table, chosen, 0.0), axis=1, keepdims=True), (LANES, LANES)
+        )
+        own_row[rows] = jnp.broadcast_to(
+            jnp.sum(jnp.where(table, info[4:5], 0.0), axis=1, keepdims=True), (LANES, LANES)
+        )
+
+    for copy in hid_copies:
+        copy.wait()
+    ain_copy.wait()
+
+    def add_u(j, carry):
+        part = jnp.dot(
+            hid[j], ain[pl.ds(pl.multiple_of(j * width, width), width), :], preferred_element_type=f32
+        )
+        u_acc[...] = jnp.where(j == 0, part, u_acc[...] + part)
+        return carry
+
+    u_acc[...] = jnp.zeros(u_acc.shape, f32)
+    lax.fori_loop(0, tiles, add_u, 0)
+    for pair in range(2):
+        rows = slice(pair * 256, (pair + 1) * 256)
+        u_buf[me, pair] = pack_rows(fold_lanes(u_acc[rows], own_row[rows]))
+    u_copies = []
+    for step in range(1, 4):
+        copy = remote(
+            u_buf.at[me],
+            u_buf.at[me],
+            u_send.at[step - 1],
+            u_recv.at[me],
+            dp=lax.rem(me + step, 4),
+        )
+        copy.start()
+        u_copies.append(copy)
+
+    def forward_z(distance):
+        @pl.when(me >= distance)
+        def _():
+            p = jnp.maximum(me - distance, 0)
+            arrived(expert, p)
+
+            @pl.when(me < 3)
+            def _():
+                to_right(p).start()
+
+            to_across(p).start()
+            to_core(expert, 0, p).start()
+
+        @pl.when(me + distance <= 3)
+        def _():
+            p = jnp.minimum(me + distance, 3)
+            arrived(expert, p)
+
+            @pl.when(me > 0)
+            def _():
+                to_left(p).start()
+
+            to_across(p).start()
+            to_core(expert, 0, p).start()
+
+    def forward_x(distance):
+        def one(p):
+            arrived(across, p)
+            to_core(across, 1, p).start()
+
+        if distance == 0:
+            one(me)
+            return
+
+        @pl.when(me >= distance)
+        def _():
+            one(jnp.maximum(me - distance, 0))
+
+        @pl.when(me + distance <= 3)
+        def _():
+            one(jnp.minimum(me + distance, 3))
+
+    def transpose_tiles(j, carry):
+        hid_t[j] = hid[j].T
+        return carry
+
+    forward_z(1)
+    forward_x(0)
+    lax.fori_loop(0, tiles, transpose_tiles, 0)
+    forward_z(2)
+    forward_x(1)
+
+    def dispatch(pair):
+        for i in range(2):
+            p = pair * 2 + i
+            arrived(core, p)
+            arrived(diagonal, p)
+            for q in range(4):
+                disp[q, pair, i * LANES : (i + 1) * LANES, :] = jnp.dot(
+                    place[p], tok[q, p], preferred_element_type=f32
+                ).astype(bf16)
+
+    def send_v(pair, slot):
+        rows = pl.ds(pl.multiple_of(pair * 256, 256), 256)
+        values = dot_nt(disp[me, pair], aup[...])
+        v_buf[me, pair] = pack_rows(fold_lanes(values, own_row[rows]))
+        copies = []
+        for step in range(1, 4):
+            copy = remote(
+                v_buf.at[me, pair],
+                v_buf.at[me, pair],
+                v_send.at[slot, step - 1],
+                v_recv.at[me, pair],
+                dp=lax.rem(me + step, 4),
+            )
+            copy.start()
+            copies.append(copy)
+        return copies
+
+    def base_tiles(pair, first, last):
+        rows = pl.ds(pl.multiple_of(pair * 256, 256), 256)
+
+        def tile(j, carry):
+            total = dot_nt(disp[0, pair], down_v[j, :, 0:768])
+            for q in range(1, 4):
+                total = total + dot_nt(disp[q, pair], down_v[j, :, q * 768 : (q + 1) * 768])
+            base[j, pair] = total
+            product = hid[j, rows, :].astype(f32) * total
+            for part in range(width // LANES):
+                score_acc[rows] += product[:, part * LANES : (part + 1) * LANES]
+            return carry
+
+        lax.fori_loop(first, last, tile, 0)
+
+    own_copy.wait()
+    score_acc[...] = jnp.zeros(score_acc.shape, f32)
+    dispatch(near)
+    aup_copy.wait()
+    v_copies = send_v(near, 0)
+    for copy in down_copies:
+        copy.wait()
+    half = tiles // 2
+    base_tiles(near, 0, half)
+    forward_z(3)
+    forward_x(2)
+    base_tiles(near, half, tiles)
+
+    for step in range(1, 4):
+        p = lax.rem(me + step, 4)
+        remote(u_buf.at[p], u_buf.at[p], u_send.at[0], u_recv.at[p], dp=p).wait_recv()
+    for pair in range(2):
+        rows = slice(pair * 256, (pair + 1) * 256)
+        total = ((u_buf[0, pair] + u_buf[1, pair]) + u_buf[2, pair]) + u_buf[3, pair]
+        total = unpack_rows(total)
+        u_sum[rows] = total
+        sc_ut[:, rows] = spread_rows(w_row[rows] * total, own_row[rows]).T.astype(bf16)
+
+    forward_x(3)
+    dispatch(far)
+    v_copies += send_v(far, 1)
+    base_tiles(far, 0, tiles)
+
+    for p in range(4):
+        rows = slice(p * LANES, (p + 1) * LANES)
+        score = jnp.sum(score_acc[rows], axis=1, keepdims=True)
+        score_out[p] = jnp.broadcast_to(
+            jnp.sum(place[p].astype(f32) * score, axis=0, keepdims=True), (8, LANES)
+        )
+    score_copies = []
+    for step in range(1, 4):
+        p = lax.rem(me + step, 4)
+        copy = remote(
+            score_out.at[p],
+            score_in.at[me],
+            score_send.at[step - 1],
+            score_recv.at[me],
+            dp=p,
+        )
+        copy.start()
+        score_copies.append(copy)
+    score_in[me] = score_out[me]
+
+    ug_v[...] = adapter_scale * jnp.dot(
+        sc_ut[...], disp[me].reshape(512, 768), preferred_element_type=f32
+    )
+    ug_copy = pltpu.make_async_copy(ug_v, ugrad_out.at[0], out_sem.at[0])
+    ug_copy.start()
+
+    for step in range(1, 4):
+        p = lax.rem(me + step, 4)
+        for pair in range(2):
+            remote(
+                v_buf.at[p, pair],
+                v_buf.at[p, pair],
+                v_send.at[0, 0],
+                v_recv.at[p, pair],
+                dp=p,
+            ).wait_recv()
+    for pair in range(2):
+        rows = slice(pair * 256, (pair + 1) * 256)
+        total = ((v_buf[0, pair] + v_buf[1, pair]) + v_buf[2, pair]) + v_buf[3, pair]
+        total = unpack_rows(total)
+        v_sum[rows] = total
+        sp_v[rows] = spread_rows(total, own_row[rows]).astype(bf16)
+        sc_v[rows] = spread_rows(w_row[rows] * total, own_row[rows]).astype(bf16)
+
+    for step in range(1, 4):
+        p = lax.rem(me + step, 4)
+        remote(score_in.at[p], score_in.at[p], score_send.at[0], score_recv.at[p], dp=p).wait_recv()
+    rows = pl.ds(pl.multiple_of(me * LANES, LANES), LANES)
+    inner = (adapter_scale / 4) * jnp.sum(u_sum[rows] * v_sum[rows], axis=1, keepdims=True)
+    inner = jnp.sum(place[me].astype(f32) * inner, axis=0, keepdims=True)
+    total = ((score_in[0] + score_in[1]) + score_in[2]) + score_in[3]
+    final_out[...] = total + inner
+    final_copies = []
+    for step in range(1, 4):
+        e = lax.rem(expert + step, 4)
+        copy = remote(
+            final_out,
+            final_in.at[expert],
+            final_send.at[step - 1],
+            final_recv.at[expert],
+            expert=e,
+        )
+        copy.start()
+        final_copies.append(copy)
+    final_in[expert] = final_out[...]
+
+    def out_down(j):
+        return pltpu.make_async_copy(
+            dg_v.at[j], dgrad_out.at[0, pl.ds(j * width, width), :], out_sem_dg.at[j]
+        )
+
+    def out_hidden(j):
+        return pltpu.make_async_copy(
+            hg_v.at[j],
+            hgrad_out.at[0, :, pl.ds(pl.multiple_of(j * width, width), width)],
+            out_sem_hg.at[j],
+        )
+
+    def finish(j, carry):
+        dg_v[j] = adapter_scale * jnp.dot(hid_t[j], sc_v[...], preferred_element_type=f32)
+        out_down(j).start()
+        extra = dot_nt(
+            sp_v[...], ain[pl.ds(pl.multiple_of(j * width, width), width), :]
+        )
+        scale = w_row[...]
+        scale = jnp.concatenate([scale] * (width // LANES), axis=1)
+        hg_v[j] = (
+            scale * (base[j].reshape(512, width) + adapter_scale * extra)
+        ).astype(bf16)
+        out_hidden(j).start()
+        return carry
+
+    lax.fori_loop(0, tiles, finish, 0)
+
+    for step in range(1, 4):
+        e = lax.rem(expert + step, 4)
+        remote(
+            final_in.at[e], final_in.at[e], final_send.at[0], final_recv.at[e], expert=e
+        ).wait_recv()
+    chosen = meta[me, 0:2, :]
+    total = jnp.zeros((2, LANES), f32)
+    for e in range(4):
+        total = total + jnp.where(chosen == float(e), final_in[e, 0:1, :], 0.0)
+    router_out[...] = total
+
+    for copy in meta_copies + u_copies + v_copies + score_copies + final_copies:
+        copy.wait_send()
+    for p in range(4):
+        to_across(p).wait_send()
+        to_core(expert, 0, p).wait_send()
+        to_core(across, 1, p).wait_send()
+
+        @pl.when((me > 0) & (me <= p))
+        def _():
+            to_left(p).wait_send()
+
+        @pl.when((me < 3) & (me >= p))
+        def _():
+            to_right(p).wait_send()
+
+    ug_copy.wait()
+    for j in range(tiles):
+        out_down(j).wait()
+        out_hidden(j).wait()
+
+
+def kernel_body(
+    output_gradient,
+    hidden,
+    down_matrix,
+    adapter_down_matrix,
+    adapter_up_matrix,
+    routes,
+    router_weight,
+    tenant,
+):
+    width = 256
+    tokens, features = output_gradient.shape
+    _, slots, units = hidden.shape
+    model = down_matrix.shape[2]
+    spread = adapter_down_matrix.shape[2]
+    tiles = units // width
+    f32 = jnp.float32
+    bf16 = jnp.bfloat16
+    dma = pltpu.SemaphoreType.DMA
+    vmem = pl.BlockSpec(memory_space=pltpu.VMEM)
+    hbm = pl.BlockSpec(memory_space=pl.ANY)
+    hgrad, dgrad, ugrad, router = pl.pallas_call(
+        functools.partial(kernel, tiles),
+        out_shape=(
+            jax.ShapeDtypeStruct(hidden.shape, bf16),
+            jax.ShapeDtypeStruct(adapter_down_matrix.shape, f32),
+            jax.ShapeDtypeStruct(adapter_up_matrix.shape, f32),
+            jax.ShapeDtypeStruct((2, tokens), f32),
+        ),
+        in_specs=[hbm] * 5 + [vmem] * 3,
+        out_specs=(hbm, hbm, hbm, vmem),
+        scratch_shapes=[
+            pltpu.VMEM((4, 4, tokens, features), bf16),
+            pltpu.VMEM((4, 2, 256, features), bf16),
+            pltpu.VMEM((tiles, width, model), bf16),
+            pltpu.VMEM((tiles, slots, width), bf16),
+            pltpu.VMEM((tiles, width, slots), bf16),
+            pltpu.VMEM((units, spread), bf16),
+            pltpu.VMEM((spread, features), bf16),
+            pltpu.VMEM((tiles, 2, 256, width), f32),
+            pltpu.VMEM((tiles, slots, width), bf16),
+            pltpu.VMEM((tiles, width, spread), f32),
+            pltpu.VMEM((spread, features), f32),
+            pltpu.VMEM((slots, spread), f32),
+            pltpu.VMEM((4, 8, LANES), f32),
+            pltpu.VMEM((4, LANES, LANES), bf16),
+            pltpu.VMEM((slots, LANES), f32),
+            pltpu.VMEM((slots, LANES), f32),
+            pltpu.VMEM((4, 2, 64, LANES), f32),
+            pltpu.VMEM((4, 2, 64, LANES), f32),
+            pltpu.VMEM((slots, LANES), f32),
+            pltpu.VMEM((slots, LANES), f32),
+            pltpu.VMEM((slots, spread), bf16),
+            pltpu.VMEM((slots, spread), bf16),
+            pltpu.VMEM((spread, slots), bf16),
+            pltpu.VMEM((slots, LANES), f32),
+            pltpu.VMEM((4, 8, LANES), f32),
+            pltpu.VMEM((4, 8, LANES), f32),
+            pltpu.VMEM((8, LANES), f32),
+            pltpu.VMEM((4, 8, LANES), f32),
+            dma((4, 4)),
+            dma((2, 4)),
+            dma((4,)),
+            dma((2, 4)),
+            dma((3,)),
+            dma((4,)),
+            dma((3,)),
+            dma((4,)),
+            dma((2, 3)),
+            dma((4, 2)),
+            dma((3,)),
+            dma((4,)),
+            dma((3,)),
+            dma((4,)),
+            dma((3,)),
+            dma((tiles,)),
+            dma((tiles,)),
+            dma((1,)),
+            dma((tiles,)),
+            dma((tiles,)),
+        ],
+        compiler_params=pltpu.CompilerParams(
+            collective_id=0, has_side_effects=True, vmem_limit_bytes=58 * 1024 * 1024
+        ),
+    )(
+        output_gradient,
+        hidden,
+        down_matrix,
+        adapter_down_matrix,
+        adapter_up_matrix,
+        routes.T,
+        router_weight.T,
+        tenant[None, :],
+    )
+    return hgrad, dgrad, ugrad, router.T
+
+
+def fitting_body(mesh, *arrays):
+    gradient, hidden, down = arrays[0], arrays[1], arrays[2]
+    fits = (
+        mesh.shape["dp"] == 4
+        and mesh.shape["expert"] == 4
+        and gradient.shape == (128, 768)
+        and hidden.shape[1] == 512
+        and hidden.shape[2] % 512 == 0
+        and hidden.shape[2] <= 2048
+        and down.shape[2] == 3072
+    )
+    return (kernel_body if fits else body)(*arrays)
+
+
 def solution(mesh):
     in_specs = (
         P(("groups", "dp"), "expert"),
@@ -193,4 +848,10 @@
         P(("groups", "expert"), None, "dp"),
         P(("groups", "dp"), None),
     )
-    return jax.shard_map(body, mesh=mesh, in_specs=in_specs, out_specs=out_specs, check_vma=False)
+    return jax.shard_map(
+        functools.partial(fitting_body, mesh),
+        mesh=mesh,
+        in_specs=in_specs,
+        out_specs=out_specs,
+        check_vma=False,
+    )

time: 165 us -> 58.6 us (0.36)
  Pallas kernels: 0 us -> 50.1 us
  waiting for transfers between devices: 49.1 us -> 0 us
  blocking collectives: 48.6 us -> 0 us
  matrix products: 33.3 us -> 0 us
  between operations: 14.8 us -> 0.65 us
  other arithmetic: 6.11 us -> 0 us
  local copies, waits for them, and re-layouts: 12.8 us -> 7.57 us
    pallas_call x0 -> x1, Pallas kernels: none -> 50.1 us  [kernel_body(): pl.pallas_call(functools.partial(kernel, tiles), out_shape=(jax.ShapeDtyp...]
    all_gather x1 -> x0, waiting for transfers between devices: 36.7 us -> none  [body(): lax.all_gather((arrived, weight_slot, owner_slot), 'dp', axis=0, tiled=True)]
    dot_general x7 -> x0, matrix products: 33.3 us -> none  [the longest x5 27.8 us: contract_matrices(): lax.dot_general(left, right, (((left_dim,), (right_dim,)), ((), ())), pre...]
    all_gather x3 -> x0, blocking collectives: 23.7 us -> none  [the longest x2 18.7 us: body(): lax.all_gather((arrived, weight_slot, owner_slot), 'dp', axis=0, tiled=True)]
    all_to_all x1 -> x0, blocking collectives: 15.8 us -> none  [body(): lax.all_to_all(outgoing, 'expert', split_axis=0, concat_axis=2, tiled=True)]
    psum x1 -> x0, waiting for transfers between devices: 12.3 us -> none  [body(): lax.psum((inner_left_factor, inner_right_factor), 'dp')]
    unnamed x1 -> x0, blocking collectives: 9.05 us -> none
    unnamed x18 -> x10, local copies, waits for them, and re-layouts: 10.8 us -> 7.57 us
  transfers between devices with their start and end apart: 2 -> 0, of which waited for: 2 -> 0; matrix products, arithmetic and copies ran while one was open for 12% -> 0% of each run, Pallas kernels for 0% -> 0%
where the time goes in v1:
time: 58.6 us; the launch traced here: 58.3 us
  Pallas kernels  50.1 us (85%)
  local copies, waits for them, and re-layouts  7.57 us (13%)
  between operations  0.65 us (1%)
    pallas_call x1, Pallas kernels, kernel_body(): pl.pallas_call(functools.partial(kernel, tiles), out_shape=(jax.ShapeDtyp...  50.1 us
    unnamed x10, local copies, waits for them, and re-layouts  7.57 us

profile of v1, /device:TPU:0, one launch (start us, length us, event | category | flops | bytes accessed | tf_op | source)
XLA Modules:
  0.0 58.3 jit_solution(14970419871545578024)
XLA Ops:
  0.6 50.1 %shard_map.111 = (bf16[1,512,2048]{2,1,0:T(8,128)(2,1)}, f32[1,2048,512]{2,1,0:T(8,128)}, f32[1,512,768]{2,1,0:T(8,128)}, f32[2,128]{1,0:T(2,128)}) custom-call(bf16[128,768]{1,0:T(8,128)(2,1)} %grad_ref.1, bf16[1,512,2048]{2,1,0:T(8,128)(2,1)} %hidden_ref.1, bf16[1,2048,3072]{2,1,0:T(8,128)(2,1)} %down_ref.1, bf16[1,2048,512]{2,1,0:T(8,128)(2,1)} %adown_ref.1, ...), custom_call_target="tpu_custom_call" | custom-call | tf_op jit(solution)/shard_map/pallas_call | solution.py:744
  50.7 0.0 copy-start
  50.8 3.3 %copy.16 = bf16[1,512,2048]{2,1,0:T(8,128)(2,1)} copy(bf16[1,512,2048]{2,1,0:T(8,128)(2,1)} %get-tuple-element.16) | data formatting | bytes 4194304
  54.1 0.0 copy-done
  54.1 0.0 copy-start.1
  54.1 2.0 %copy.17 = f32[1,2048,512]{2,1,0:T(8,128)} copy(f32[1,2048,512]{2,1,0:T(8,128)S(1)} %copy-done) | data formatting | bytes 8388608
  56.1 0.5 copy-done.1
  56.6 0.0 copy-start.2
  56.6 1.1 %copy.18 = f32[1,512,768]{2,1,0:T(8,128)} copy(f32[1,512,768]{2,1,0:T(8,128)S(1)} %copy-done.1) | data formatting | bytes 3145728
  57.8 0.0 copy-done.2
  57.8 0.6 copy.19
Async XLA Ops:
  50.7 3.3 %copy-start = (f32[1,2048,512]{2,1,0:T(8,128)S(1)}, f32[1,2048,512]{2,1,0:T(8,128)}, u32[]{:S(2)}) copy-start(f32[1,2048,512]{2,1,0:T(8,128)} %get-tuple-element.17) | copy-start | bytes 12582916
  54.1 2.5 %copy-start.1 = (f32[1,512,768]{2,1,0:T(8,128)S(1)}, f32[1,512,768]{2,1,0:T(8,128)}, u32[]{:S(2)}) copy-start(f32[1,512,768]{2,1,0:T(8,128)} %get-tuple-element.18) | copy-start | bytes 4718596
  56.6 1.1 %copy-start.2 = (f32[2,128]{1,0:T(2,128)S(1)}, f32[2,128]{1,0:T(2,128)}, u32[]{:S(2)}) copy-start(f32[2,128]{1,0:T(2,128)} %get-tuple-element.11) | copy-start | bytes 3076

commit v2 on v1

--- a/solution.py
+++ b/solution.py
@@ -238,8 +238,10 @@
     weight_ref,
     tenant_ref,
     hgrad_out,
-    dgrad_out,
-    ugrad_out,
+    turned_out,
+    sc_v_out,
+    sc_ut_out,
+    feat_out,
     router_out,
     tok,
     disp,
@@ -250,8 +252,6 @@
     aup,
     base,
     hg_v,
-    dg_v,
-    ug_v,
     u_acc,
     meta,
     place,
@@ -267,8 +267,6 @@
     score_acc,
     score_out,
     score_in,
-    final_out,
-    final_in,
     tok_recv,
     send_z,
     send_x,
@@ -281,14 +279,11 @@
     v_recv,
     score_send,
     score_recv,
-    final_send,
-    final_recv,
     load_sem,
     down_sem,
     hid_sem,
     out_sem,
     out_sem_hg,
-    out_sem_dg,
 ):
     me = lax.axis_index("dp")
     expert = lax.axis_index("expert")
@@ -329,14 +324,17 @@
     meta[me, 5:8, :] = jnp.zeros((3, LANES), f32)
 
     barrier = pltpu.get_barrier_semaphore()
-    for step in range(1, 4):
+    for step in range(1, 16):
         pl.semaphore_signal(
-            barrier, inc=1, device_id={"dp": lax.rem(me + step, 4)}, device_id_type=MESH
-        )
-        pl.semaphore_signal(
-            barrier, inc=1, device_id={"expert": lax.rem(expert + step, 4)}, device_id_type=MESH
-        )
-    pl.semaphore_wait(barrier, 6)
+            barrier,
+            inc=1,
+            device_id={
+                "dp": lax.rem(me + step // 4, 4),
+                "expert": lax.rem(expert + step % 4, 4),
+            },
+            device_id_type=MESH,
+        )
+    pl.semaphore_wait(barrier, 15)
 
     def remote(src, dst, send, recv, **target):
         return pltpu.make_async_remote_copy(
@@ -460,17 +458,6 @@
     for pair in range(2):
         rows = slice(pair * 256, (pair + 1) * 256)
         u_buf[me, pair] = pack_rows(fold_lanes(u_acc[rows], own_row[rows]))
-    u_copies = []
-    for step in range(1, 4):
-        copy = remote(
-            u_buf.at[me],
-            u_buf.at[me],
-            u_send.at[step - 1],
-            u_recv.at[me],
-            dp=lax.rem(me + step, 4),
-        )
-        copy.start()
-        u_copies.append(copy)
 
     def forward_z(distance):
         @pl.when(me >= distance)
@@ -521,6 +508,8 @@
     forward_z(1)
     forward_x(0)
     lax.fori_loop(0, tiles, transpose_tiles, 0)
+    turned_copy = pltpu.make_async_copy(hid_t, turned_out, out_sem.at[0])
+    turned_copy.start()
     forward_z(2)
     forward_x(1)
 
@@ -534,10 +523,13 @@
                     place[p], tok[q, p], preferred_element_type=f32
                 ).astype(bf16)
 
-    def send_v(pair, slot):
+    def make_v(pair):
         rows = pl.ds(pl.multiple_of(pair * 256, 256), 256)
         values = dot_nt(disp[me, pair], aup[...])
-        v_buf[me, pair] = pack_rows(fold_lanes(values, own_row[rows]))
+        v_sum[rows] = fold_lanes(values, own_row[rows])
+        v_buf[me, pair] = pack_rows(v_sum[rows])
+
+    def send_v(pair, slot):
         copies = []
         for step in range(1, 4):
             copy = remote(
@@ -570,14 +562,34 @@
     score_acc[...] = jnp.zeros(score_acc.shape, f32)
     dispatch(near)
     aup_copy.wait()
-    v_copies = send_v(near, 0)
+    make_v(near)
     for copy in down_copies:
         copy.wait()
     half = tiles // 2
     base_tiles(near, 0, half)
     forward_z(3)
+    v_copies = send_v(near, 0)
+    u_copies = []
+    for step in range(1, 4):
+        copy = remote(
+            u_buf.at[me],
+            u_buf.at[me],
+            u_send.at[step - 1],
+            u_recv.at[me],
+            dp=lax.rem(me + step, 4),
+        )
+        copy.start()
+        u_copies.append(copy)
     forward_x(2)
     base_tiles(near, half, tiles)
+
+    forward_x(3)
+    dispatch(far)
+    make_v(far)
+    v_copies += send_v(far, 1)
+    feat_copy = pltpu.make_async_copy(disp.at[me], feat_out, out_sem.at[1])
+    feat_copy.start()
+    base_tiles(far, 0, tiles)
 
     for step in range(1, 4):
         p = lax.rem(me + step, 4)
@@ -588,37 +600,28 @@
         total = unpack_rows(total)
         u_sum[rows] = total
         sc_ut[:, rows] = spread_rows(w_row[rows] * total, own_row[rows]).T.astype(bf16)
-
-    forward_x(3)
-    dispatch(far)
-    v_copies += send_v(far, 1)
-    base_tiles(far, 0, tiles)
-
+    sc_ut_copy = pltpu.make_async_copy(sc_ut, sc_ut_out, out_sem.at[2])
+    sc_ut_copy.start()
+
+    score_acc[...] += (adapter_scale / 4) * u_sum[...] * v_sum[...]
     for p in range(4):
         rows = slice(p * LANES, (p + 1) * LANES)
         score = jnp.sum(score_acc[rows], axis=1, keepdims=True)
-        score_out[p] = jnp.broadcast_to(
-            jnp.sum(place[p].astype(f32) * score, axis=0, keepdims=True), (8, LANES)
-        )
+        score_out[p] = jnp.sum(place[p].astype(f32) * score, axis=0, keepdims=True)
     score_copies = []
-    for step in range(1, 4):
-        p = lax.rem(me + step, 4)
+    for step in range(1, 16):
+        p = lax.rem(me + step // 4, 4)
         copy = remote(
             score_out.at[p],
-            score_in.at[me],
+            score_in.at[me, expert],
             score_send.at[step - 1],
-            score_recv.at[me],
+            score_recv.at[me, expert],
             dp=p,
+            expert=lax.rem(expert + step % 4, 4),
         )
         copy.start()
         score_copies.append(copy)
-    score_in[me] = score_out[me]
-
-    ug_v[...] = adapter_scale * jnp.dot(
-        sc_ut[...], disp[me].reshape(512, 768), preferred_element_type=f32
-    )
-    ug_copy = pltpu.make_async_copy(ug_v, ugrad_out.at[0], out_sem.at[0])
-    ug_copy.start()
+    score_in[me, expert] = score_out[me]
 
     for step in range(1, 4):
         p = lax.rem(me + step, 4)
@@ -634,47 +637,16 @@
         rows = slice(pair * 256, (pair + 1) * 256)
         total = ((v_buf[0, pair] + v_buf[1, pair]) + v_buf[2, pair]) + v_buf[3, pair]
         total = unpack_rows(total)
-        v_sum[rows] = total
         sp_v[rows] = spread_rows(total, own_row[rows]).astype(bf16)
         sc_v[rows] = spread_rows(w_row[rows] * total, own_row[rows]).astype(bf16)
 
-    for step in range(1, 4):
-        p = lax.rem(me + step, 4)
-        remote(score_in.at[p], score_in.at[p], score_send.at[0], score_recv.at[p], dp=p).wait_recv()
-    rows = pl.ds(pl.multiple_of(me * LANES, LANES), LANES)
-    inner = (adapter_scale / 4) * jnp.sum(u_sum[rows] * v_sum[rows], axis=1, keepdims=True)
-    inner = jnp.sum(place[me].astype(f32) * inner, axis=0, keepdims=True)
-    total = ((score_in[0] + score_in[1]) + score_in[2]) + score_in[3]
-    final_out[...] = total + inner
-    final_copies = []
-    for step in range(1, 4):
-        e = lax.rem(expert + step, 4)
-        copy = remote(
-            final_out,
-            final_in.at[expert],
-            final_send.at[step - 1],
-            final_recv.at[expert],
-            expert=e,
-        )
-        copy.start()
-        final_copies.append(copy)
-    final_in[expert] = final_out[...]
-
-    def out_down(j):
-        return pltpu.make_async_copy(
-            dg_v.at[j], dgrad_out.at[0, pl.ds(j * width, width), :], out_sem_dg.at[j]
-        )
+    sc_v_copy = pltpu.make_async_copy(sc_v, sc_v_out, out_sem.at[3])
+    sc_v_copy.start()
 
     def out_hidden(j):
-        return pltpu.make_async_copy(
-            hg_v.at[j],
-            hgrad_out.at[0, :, pl.ds(pl.multiple_of(j * width, width), width)],
-            out_sem_hg.at[j],
-        )
+        return pltpu.make_async_copy(hg_v.at[j], hgrad_out.at[j], out_sem_hg.at[j])
 
     def finish(j, carry):
-        dg_v[j] = adapter_scale * jnp.dot(hid_t[j], sc_v[...], preferred_element_type=f32)
-        out_down(j).start()
         extra = dot_nt(
             sp_v[...], ain[pl.ds(pl.multiple_of(j * width, width), width), :]
         )
@@ -688,18 +660,21 @@
 
     lax.fori_loop(0, tiles, finish, 0)
 
-    for step in range(1, 4):
-        e = lax.rem(expert + step, 4)
+    for step in range(1, 16):
+        p = lax.rem(me + step // 4, 4)
+        e = lax.rem(expert + step % 4, 4)
+        block = score_in.at[p, e]
         remote(
-            final_in.at[e], final_in.at[e], final_send.at[0], final_recv.at[e], expert=e
+            block, block, score_send.at[0], score_recv.at[p, e], dp=p, expert=e
         ).wait_recv()
     chosen = meta[me, 0:2, :]
     total = jnp.zeros((2, LANES), f32)
     for e in range(4):
-        total = total + jnp.where(chosen == float(e), final_in[e, 0:1, :], 0.0)
+        score = ((score_in[0, e] + score_in[1, e]) + score_in[2, e]) + score_in[3, e]
+        total = total + jnp.where(chosen == float(e), score, 0.0)
     router_out[...] = total
 
-    for copy in meta_copies + u_copies + v_copies + score_copies + final_copies:
+    for copy in meta_copies + u_copies + v_copies + score_copies:
         copy.wait_send()
     for p in range(4):
         to_across(p).wait_send()
@@ -714,10 +689,25 @@
         def _():
             to_right(p).wait_send()
 
-    ug_copy.wait()
+    turned_copy.wait()
+    feat_copy.wait()
+    sc_ut_copy.wait()
+    sc_v_copy.wait()
     for j in range(tiles):
-        out_down(j).wait()
         out_hidden(j).wait()
+
+
+def products_kernel(hg, turned, scaled_v, scaled_ut, feat, router, hgrad, dgrad, ugrad, router_out):
+    width = turned.shape[1]
+    for part in range(turned.shape[0]):
+        hgrad[0, :, part * width : (part + 1) * width] = hg[part]
+        dgrad[0, part * width : (part + 1) * width, :] = adapter_scale * jnp.dot(
+            turned[part], scaled_v[...], preferred_element_type=jnp.float32
+        )
+    ugrad[0] = adapter_scale * jnp.dot(
+        scaled_ut[...], feat[...], preferred_element_type=jnp.float32
+    )
+    router_out[...] = router[...]
 
 
 def kernel_body(
@@ -741,16 +731,18 @@
     dma = pltpu.SemaphoreType.DMA
     vmem = pl.BlockSpec(memory_space=pltpu.VMEM)
     hbm = pl.BlockSpec(memory_space=pl.ANY)
-    hgrad, dgrad, ugrad, router = pl.pallas_call(
+    hg, turned, scaled_v, scaled_ut, feat, router = pl.pallas_call(
         functools.partial(kernel, tiles),
         out_shape=(
-            jax.ShapeDtypeStruct(hidden.shape, bf16),
-            jax.ShapeDtypeStruct(adapter_down_matrix.shape, f32),
-            jax.ShapeDtypeStruct(adapter_up_matrix.shape, f32),
+            jax.ShapeDtypeStruct((tiles, slots, width), bf16),
+            jax.ShapeDtypeStruct((tiles, width, slots), bf16),
+            jax.ShapeDtypeStruct((slots, spread), bf16),
+            jax.ShapeDtypeStruct((spread, slots), bf16),
+            jax.ShapeDtypeStruct((2, 256, features), bf16),
             jax.ShapeDtypeStruct((2, tokens), f32),
         ),
         in_specs=[hbm] * 5 + [vmem] * 3,
-        out_specs=(hbm, hbm, hbm, vmem),
+        out_specs=(hbm, hbm, hbm, hbm, hbm, vmem),
         scratch_shapes=[
             pltpu.VMEM((4, 4, tokens, features), bf16),
             pltpu.VMEM((4, 2, 256, features), bf16),
@@ -761,8 +753,6 @@
             pltpu.VMEM((spread, features), bf16),
             pltpu.VMEM((tiles, 2, 256, width), f32),
             pltpu.VMEM((tiles, slots, width), bf16),
-            pltpu.VMEM((tiles, width, spread), f32),
-            pltpu.VMEM((spread, features), f32),
             pltpu.VMEM((slots, spread), f32),
             pltpu.VMEM((4, 8, LANES), f32),
             pltpu.VMEM((4, LANES, LANES), bf16),
@@ -776,10 +766,8 @@
             pltpu.VMEM((slots, spread), bf16),
             pltpu.VMEM((spread, slots), bf16),
             pltpu.VMEM((slots, LANES), f32),
-            pltpu.VMEM((4, 8, LANES), f32),
-            pltpu.VMEM((4, 8, LANES), f32),
-            pltpu.VMEM((8, LANES), f32),
-            pltpu.VMEM((4, 8, LANES), f32),
+            pltpu.VMEM((4, 1, LANES), f32),
+            pltpu.VMEM((4, 4, 1, LANES), f32),
             dma((4, 4)),
             dma((2, 4)),
             dma((4,)),
@@ -790,15 +778,12 @@
             dma((4,)),
             dma((2, 3)),
             dma((4, 2)),
-            dma((3,)),
-            dma((4,)),
-            dma((3,)),
-            dma((4,)),
+            dma((15,)),
+            dma((4, 4)),
             dma((3,)),
             dma((tiles,)),
             dma((tiles,)),
-            dma((1,)),
-            dma((tiles,)),
+            dma((4,)),
             dma((tiles,)),
         ],
         compiler_params=pltpu.CompilerParams(
@@ -814,6 +799,34 @@
         router_weight.T,
         tenant[None, :],
     )
+    group = 2
+    steps = tiles // group
+    whole = lambda j: (0, 0)
+    hgrad, dgrad, ugrad, router = pl.pallas_call(
+        products_kernel,
+        grid=(steps,),
+        out_shape=(
+            jax.ShapeDtypeStruct(hidden.shape, bf16),
+            jax.ShapeDtypeStruct(adapter_down_matrix.shape, f32),
+            jax.ShapeDtypeStruct(adapter_up_matrix.shape, f32),
+            jax.ShapeDtypeStruct((2, tokens), f32),
+        ),
+        in_specs=[
+            pl.BlockSpec((group, slots, width), lambda j: (j, 0, 0)),
+            pl.BlockSpec((group, width, slots), lambda j: (j, 0, 0)),
+            pl.BlockSpec((slots, spread), whole),
+            pl.BlockSpec((spread // steps, slots), lambda j: (j, 0)),
+            pl.BlockSpec((slots, features), whole),
+            pl.BlockSpec((2, tokens), whole),
+        ],
+        out_specs=(
+            pl.BlockSpec((1, slots, group * width), lambda j: (0, 0, j)),
+            pl.BlockSpec((1, group * width, spread), lambda j: (0, j, 0)),
+            pl.BlockSpec((1, spread // steps, features), lambda j: (0, j, 0)),
+            pl.BlockSpec((2, tokens), whole),
+        ),
+        compiler_params=pltpu.CompilerParams(vmem_limit_bytes=58 * 1024 * 1024),
+    )(hg, turned, scaled_v, scaled_ut, feat.reshape(slots, features), router)
     return hgrad, dgrad, ugrad, router.T
 
 
@@ -824,8 +837,7 @@
         and mesh.shape["expert"] == 4
         and gradient.shape == (128, 768)
         and hidden.shape[1] == 512
-        and hidden.shape[2] % 512 == 0
-        and hidden.shape[2] <= 2048
+        and hidden.shape[2] == 2048
         and down.shape[2] == 3072
     )
     return (kernel_body if fits else body)(*arrays)

time: 58.6 us -> 52.4 us (0.89)
  local copies, waits for them, and re-layouts: 7.57 us -> 0 us
  Pallas kernels: 50.1 us -> 51.6 us
    unnamed x10 -> x0, local copies, waits for them, and re-layouts: 7.57 us -> none
    pallas_call x0 -> x1, Pallas kernels: none -> 7.14 us  [kernel_body(): pl.pallas_call(products_kernel, grid=(steps,), out_shape=(jax.ShapeDtypeS...]
    pallas_call x1, Pallas kernels: 50.1 us -> 44.4 us  [kernel_body(): pl.pallas_call(functools.partial(kernel, tiles), out_shape=(jax.ShapeDtyp...]
where the time goes in v2:
time: 52.4 us; the launch traced here: 52.2 us
  Pallas kernels  51.6 us (98%)
  between operations  0.64 us (1%)
    pallas_call x1, Pallas kernels, kernel_body(): pl.pallas_call(functools.partial(kernel, tiles), out_shape=(jax.ShapeDtyp...  44.4 us
    pallas_call x1, Pallas kernels, kernel_body(): pl.pallas_call(products_kernel, grid=(steps,), out_shape=(jax.ShapeDtypeS...  7.14 us

profile of v2, /device:TPU:0, one launch (start us, length us, event | category | flops | bytes accessed | tf_op | source)
XLA Modules:
  0.0 52.2 jit_solution(2858200295200557136)
XLA Ops:
  0.6 44.4 %shard_map.111 = (bf16[8,512,256]{2,1,0:T(8,128)(2,1)}, bf16[8,256,512]{2,1,0:T(8,128)(2,1)}, bf16[512,512]{1,0:T(8,128)(2,1)}, bf16[512,512]{1,0:T(8,128)(2,1)}...) custom-call(bf16[128,768]{1,0:T(8,128)(2,1)} %grad_ref.1, bf16[1,512,2048]{2,1,0:T(8,128)(2,1)} %hidden_ref.1, ...), custom_call_target="tpu_custom_call" | custom-call | tf_op jit(solution)/shard_map/pallas_call | solution.py:734
  45.1 7.1 %shard_map.112 = (bf16[1,512,2048]{2,1,0:T(8,128)(2,1)}, f32[1,2048,512]{2,1,0:T(8,128)}, f32[1,512,768]{2,1,0:T(8,128)}, f32[2,128]{1,0:T(2,128)}) custom-call(bf16[8,512,256]{2,1,0:T(8,128)(2,1)} %get-tuple-element.14.hg, bf16[8,256,512]{2,1,0:T(8,128)(2,1)} %get-tuple-element.15.turned, bf16[512,512]{1,0:T(8,128)(2,1)} %get-tuple-element.16.scaled_v, ...), custom_call_target="tpu_custom_call" | custom-call | tf_op jit(solution)/shard_map/pallas_call | solution.py:805

commit v3 on v2

--- a/solution.py
+++ b/solution.py
@@ -182,6 +182,7 @@
 
 MESH = pl.DeviceIdType.MESH
 LANES = 128
+CHUNKS = 4
 
 
 def dot_nt(left, right):
@@ -346,49 +347,31 @@
             device_id_type=MESH,
         )
 
-    def to_left(p, src=None):
-        block = tok.at[expert, p]
+    chunk_rows = tok.shape[2] // CHUNKS
+
+    def chunk(ref, i):
+        return ref.at[pl.ds(i * chunk_rows, chunk_rows)]
+
+    def send(i, q, p, src, sent, **target):
+        block = chunk(tok.at[q, p], i)
         return remote(
-            block if src is None else src,
-            block,
-            send_z.at[0, p],
-            tok_recv.at[expert, p],
-            dp=jnp.maximum(me - 1, 0),
-        )
-
-    def to_right(p, src=None):
-        block = tok.at[expert, p]
-        return remote(
-            block if src is None else src,
-            block,
-            send_z.at[1, p],
-            tok_recv.at[expert, p],
-            dp=jnp.minimum(me + 1, 3),
-        )
-
-    def to_across(p, src=None):
-        block = tok.at[expert, p]
-        return remote(
-            block if src is None else src,
-            block,
-            send_x.at[p],
-            tok_recv.at[expert, p],
-            expert=across,
-        )
-
-    def to_core(q, slot, p, src=None):
-        block = tok.at[q, p]
-        return remote(
-            block if src is None else src,
-            block,
-            send_c.at[slot, p],
-            tok_recv.at[q, p],
-            expert=core,
-        )
-
-    def arrived(q, p):
-        block = tok.at[q, p]
-        remote(block, block, send_c.at[0, p], tok_recv.at[q, p], expert=core).wait_recv()
+            block if src is None else chunk(src, i), block, sent, tok_recv.at[q, p, i], **target
+        )
+
+    def to_left(i, p, src=None):
+        return send(i, expert, p, src, send_z.at[0, p, i], dp=jnp.maximum(me - 1, 0))
+
+    def to_right(i, p, src=None):
+        return send(i, expert, p, src, send_z.at[1, p, i], dp=jnp.minimum(me + 1, 3))
+
+    def to_across(i, p, src=None):
+        return send(i, expert, p, src, send_x.at[p, i], expert=across)
+
+    def to_core(i, q, slot, p, src=None):
+        return send(i, q, p, src, send_c.at[slot, p, i], expert=core)
+
+    def arrived(i, q, p):
+        send(i, q, p, None, send_c.at[0, p, i], expert=core).wait_recv()
 
     meta_copies = []
     for step in range(1, 4):
@@ -402,17 +385,79 @@
         copy.start()
         meta_copies.append(copy)
 
-    @pl.when(me > 0)
-    def _():
-        to_left(me, grad_ref).start()
-
-    @pl.when(me < 3)
-    def _():
-        to_right(me, grad_ref).start()
-
-    to_across(me, grad_ref).start()
-    to_core(expert, 0, me, grad_ref).start()
-
+    for i in range(CHUNKS):
+
+        @pl.when(me > 0)
+        def _():
+            to_left(i, me, grad_ref).start()
+
+        @pl.when(me < 3)
+        def _():
+            to_right(i, me, grad_ref).start()
+
+        to_across(i, me, grad_ref).start()
+    for i in range(CHUNKS):
+        to_core(i, expert, 0, me, grad_ref).start()
+
+    def forward_z(i, distance):
+        @pl.when(me >= distance)
+        def _():
+            p = jnp.maximum(me - distance, 0)
+            arrived(i, expert, p)
+
+            @pl.when(me < 3)
+            def _():
+                to_right(i, p).start()
+
+            to_across(i, p).start()
+            to_core(i, expert, 0, p).start()
+
+        @pl.when(me + distance <= 3)
+        def _():
+            p = jnp.minimum(me + distance, 3)
+            arrived(i, expert, p)
+
+            @pl.when(me > 0)
+            def _():
+                to_left(i, p).start()
+
+            to_across(i, p).start()
+            to_core(i, expert, 0, p).start()
+
+    def forward_x(i, distance):
+        def one(p):
+            arrived(i, across, p)
+            to_core(i, across, 1, p).start()
+
+        if distance == 0:
+            one(me)
+            return
+
+        @pl.when(me >= distance)
+        def _():
+            one(jnp.maximum(me - distance, 0))
+
+        @pl.when(me + distance <= 3)
+        def _():
+            one(jnp.minimum(me + distance, 3))
+
+    def forward(distance):
+        for i in range(CHUNKS):
+            if distance <= 3:
+                forward_z(i, distance)
+            forward_x(i, distance - 1)
+
+    for copy in hid_copies:
+        copy.wait()
+
+    def transpose_tiles(j, carry):
+        hid_t[j] = hid[j].T
+        return carry
+
+    lax.fori_loop(0, tiles, transpose_tiles, 0)
+    turned_copy = pltpu.make_async_copy(hid_t, turned_out, out_sem.at[0])
+    turned_copy.start()
+    forward(1)
     for step in range(1, 4):
         p = lax.rem(me + step, 4)
         remote(
@@ -442,8 +487,8 @@
             jnp.sum(jnp.where(table, info[4:5], 0.0), axis=1, keepdims=True), (LANES, LANES)
         )
 
-    for copy in hid_copies:
-        copy.wait()
+    forward(2)
+
     ain_copy.wait()
 
     def add_u(j, carry):
@@ -459,65 +504,13 @@
         rows = slice(pair * 256, (pair + 1) * 256)
         u_buf[me, pair] = pack_rows(fold_lanes(u_acc[rows], own_row[rows]))
 
-    def forward_z(distance):
-        @pl.when(me >= distance)
-        def _():
-            p = jnp.maximum(me - distance, 0)
-            arrived(expert, p)
-
-            @pl.when(me < 3)
-            def _():
-                to_right(p).start()
-
-            to_across(p).start()
-            to_core(expert, 0, p).start()
-
-        @pl.when(me + distance <= 3)
-        def _():
-            p = jnp.minimum(me + distance, 3)
-            arrived(expert, p)
-
-            @pl.when(me > 0)
-            def _():
-                to_left(p).start()
-
-            to_across(p).start()
-            to_core(expert, 0, p).start()
-
-    def forward_x(distance):
-        def one(p):
-            arrived(across, p)
-            to_core(across, 1, p).start()
-
-        if distance == 0:
-            one(me)
-            return
-
-        @pl.when(me >= distance)
-        def _():
-            one(jnp.maximum(me - distance, 0))
-
-        @pl.when(me + distance <= 3)
-        def _():
-            one(jnp.minimum(me + distance, 3))
-
-    def transpose_tiles(j, carry):
-        hid_t[j] = hid[j].T
-        return carry
-
-    forward_z(1)
-    forward_x(0)
-    lax.fori_loop(0, tiles, transpose_tiles, 0)
-    turned_copy = pltpu.make_async_copy(hid_t, turned_out, out_sem.at[0])
-    turned_copy.start()
-    forward_z(2)
-    forward_x(1)
 
     def dispatch(pair):
         for i in range(2):
             p = pair * 2 + i
-            arrived(core, p)
-            arrived(diagonal, p)
+            for j in range(CHUNKS):
+                arrived(j, core, p)
+                arrived(j, diagonal, p)
             for q in range(4):
                 disp[q, pair, i * LANES : (i + 1) * LANES, :] = jnp.dot(
                     place[p], tok[q, p], preferred_element_type=f32
@@ -558,17 +551,7 @@
 
         lax.fori_loop(first, last, tile, 0)
 
-    own_copy.wait()
-    score_acc[...] = jnp.zeros(score_acc.shape, f32)
-    dispatch(near)
-    aup_copy.wait()
-    make_v(near)
-    for copy in down_copies:
-        copy.wait()
-    half = tiles // 2
-    base_tiles(near, 0, half)
-    forward_z(3)
-    v_copies = send_v(near, 0)
+    forward(3)
     u_copies = []
     for step in range(1, 4):
         copy = remote(
@@ -580,10 +563,16 @@
         )
         copy.start()
         u_copies.append(copy)
-    forward_x(2)
-    base_tiles(near, half, tiles)
-
-    forward_x(3)
+    own_copy.wait()
+    score_acc[...] = jnp.zeros(score_acc.shape, f32)
+    dispatch(near)
+    aup_copy.wait()
+    make_v(near)
+    v_copies = send_v(near, 0)
+    for copy in down_copies:
+        copy.wait()
+    base_tiles(near, 0, tiles)
+    forward(4)
     dispatch(far)
     make_v(far)
     v_copies += send_v(far, 1)
@@ -677,17 +666,18 @@
     for copy in meta_copies + u_copies + v_copies + score_copies:
         copy.wait_send()
     for p in range(4):
-        to_across(p).wait_send()
-        to_core(expert, 0, p).wait_send()
-        to_core(across, 1, p).wait_send()
-
-        @pl.when((me > 0) & (me <= p))
-        def _():
-            to_left(p).wait_send()
-
-        @pl.when((me < 3) & (me >= p))
-        def _():
-            to_right(p).wait_send()
+        for i in range(CHUNKS):
+            to_across(i, p).wait_send()
+            to_core(i, expert, 0, p).wait_send()
+            to_core(i, across, 1, p).wait_send()
+
+            @pl.when((me > 0) & (me <= p))
+            def _():
+                to_left(i, p).wait_send()
+
+            @pl.when((me < 3) & (me >= p))
+            def _():
+                to_right(i, p).wait_send()
 
     turned_copy.wait()
     feat_copy.wait()
@@ -768,10 +758,10 @@
             pltpu.VMEM((slots, LANES), f32),
             pltpu.VMEM((4, 1, LANES), f32),
             pltpu.VMEM((4, 4, 1, LANES), f32),
-            dma((4, 4)),
-            dma((2, 4)),
-            dma((4,)),
-            dma((2, 4)),
+            dma((4, 4, CHUNKS)),
+            dma((2, 4, CHUNKS)),
+            dma((4, CHUNKS)),
+            dma((2, 4, CHUNKS)),
             dma((3,)),
             dma((4,)),
             dma((3,)),

time: 52.4 us -> 52.7 us (level)
  no operation moved by 1% of the time
where the time goes in v3:
time: 52.7 us; the launch traced here: 52.5 us
  Pallas kernels  51.8 us (98%)
  between operations  0.64 us (1%)
    pallas_call x1, Pallas kernels, kernel_body(): pl.pallas_call(functools.partial(kernel, tiles), out_shape=(jax.ShapeDtyp...  44.7 us
    pallas_call x1, Pallas kernels, kernel_body(): pl.pallas_call(products_kernel, grid=(steps,), out_shape=(jax.ShapeDtypeS...  7.14 us

profile of v3, /device:TPU:0, one launch (start us, length us, event | category | flops | bytes accessed | tf_op | source)
XLA Modules:
  0.0 52.5 jit_solution(7664261431918368910)
XLA Ops:
  0.6 44.7 %shard_map.111 = (bf16[8,512,256]{2,1,0:T(8,128)(2,1)}, bf16[8,256,512]{2,1,0:T(8,128)(2,1)}, bf16[512,512]{1,0:T(8,128)(2,1)}, bf16[512,512]{1,0:T(8,128)(2,1)}...) custom-call(bf16[128,768]{1,0:T(8,128)(2,1)} %grad_ref.1, bf16[1,512,2048]{2,1,0:T(8,128)(2,1)} %hidden_ref.1, ...), custom_call_target="tpu_custom_call" | custom-call | tf_op jit(solution)/shard_map/pallas_call | solution.py:724
  45.3 7.1 %shard_map.112 = (bf16[1,512,2048]{2,1,0:T(8,128)(2,1)}, f32[1,2048,512]{2,1,0:T(8,128)}, f32[1,512,768]{2,1,0:T(8,128)}, f32[2,128]{1,0:T(2,128)}) custom-call(bf16[8,512,256]{2,1,0:T(8,128)(2,1)} %get-tuple-element.14.hg, bf16[8,256,512]{2,1,0:T(8,128)(2,1)} %get-tuple-element.15.turned, bf16[512,512]{1,0:T(8,128)(2,1)} %get-tuple-element.16.scaled_v, ...), custom_call_target="tpu_custom_call" | custom-call | tf_op jit(solution)/shard_map/pallas_call | solution.py:795

commit v4 on v3

--- a/solution.py
+++ b/solution.py
@@ -572,14 +572,6 @@
     for copy in down_copies:
         copy.wait()
     base_tiles(near, 0, tiles)
-    forward(4)
-    dispatch(far)
-    make_v(far)
-    v_copies += send_v(far, 1)
-    feat_copy = pltpu.make_async_copy(disp.at[me], feat_out, out_sem.at[1])
-    feat_copy.start()
-    base_tiles(far, 0, tiles)
-
     for step in range(1, 4):
         p = lax.rem(me + step, 4)
         remote(u_buf.at[p], u_buf.at[p], u_send.at[0], u_recv.at[p], dp=p).wait_recv()
@@ -591,6 +583,14 @@
         sc_ut[:, rows] = spread_rows(w_row[rows] * total, own_row[rows]).T.astype(bf16)
     sc_ut_copy = pltpu.make_async_copy(sc_ut, sc_ut_out, out_sem.at[2])
     sc_ut_copy.start()
+
+    forward(4)
+    dispatch(far)
+    make_v(far)
+    v_copies += send_v(far, 1)
+    feat_copy = pltpu.make_async_copy(disp.at[me], feat_out, out_sem.at[1])
+    feat_copy.start()
+    base_tiles(far, 0, tiles)
 
     score_acc[...] += (adapter_scale / 4) * u_sum[...] * v_sum[...]
     for p in range(4):
@@ -789,7 +789,7 @@
         router_weight.T,
         tenant[None, :],
     )
-    group = 2
+    group = 1
     steps = tiles // group
     whole = lambda j: (0, 0)
     hgrad, dgrad, ugrad, router = pl.pallas_call(

time: 52.7 us -> 57.2 us (1.085)
  Pallas kernels: 51.8 us -> 56.3 us
    pallas_call x1, Pallas kernels: 44.7 us -> 47.4 us  [kernel_body(): pl.pallas_call(functools.partial(kernel, tiles), out_shape=(jax.ShapeDtyp...]
    pallas_call x1, Pallas kernels: 7.14 us -> 8.91 us  [kernel_body(): pl.pallas_call(products_kernel, grid=(steps,), out_shape=(jax.ShapeDtypeS...]
where the time goes in v4:
time: 57.2 us; the launch traced here: 56.9 us
  Pallas kernels  56.3 us (98%)
  between operations  0.64 us (1%)
    pallas_call x1, Pallas kernels, kernel_body(): pl.pallas_call(functools.partial(kernel, tiles), out_shape=(jax.ShapeDtyp...  47.4 us
    pallas_call x1, Pallas kernels, kernel_body(): pl.pallas_call(products_kernel, grid=(steps,), out_shape=(jax.ShapeDtypeS...  8.91 us

profile of v4, /device:TPU:0, one launch (start us, length us, event | category | flops | bytes accessed | tf_op | source)
XLA Modules:
  0.0 56.9 jit_solution(14283757817068417486)
XLA Ops:
  0.6 47.4 %shard_map.111 = (bf16[8,512,256]{2,1,0:T(8,128)(2,1)}, bf16[8,256,512]{2,1,0:T(8,128)(2,1)}, bf16[512,512]{1,0:T(8,128)(2,1)}, bf16[512,512]{1,0:T(8,128)(2,1)}...) custom-call(bf16[128,768]{1,0:T(8,128)(2,1)} %grad_ref.1, bf16[1,512,2048]{2,1,0:T(8,128)(2,1)} %hidden_ref.1, ...), custom_call_target="tpu_custom_call" | custom-call | tf_op jit(solution)/shard_map/pallas_call | solution.py:724
  48.0 8.9 %shard_map.112 = (bf16[1,512,2048]{2,1,0:T(8,128)(2,1)}, f32[1,2048,512]{2,1,0:T(8,128)}, f32[1,512,768]{2,1,0:T(8,128)}, f32[2,128]{1,0:T(2,128)}) custom-call(bf16[8,512,256]{2,1,0:T(8,128)(2,1)} %get-tuple-element.14.hg, bf16[8,256,512]{2,1,0:T(8,128)(2,1)} %get-tuple-element.15.turned, bf16[512,512]{1,0:T(8,128)(2,1)} %get-tuple-element.16.scaled_v, ...), custom_call_target="tpu_custom_call" | custom-call | tf_op jit(solution)/shard_map/pallas_call | solution.py:795
